TPU v7x, 32 devices: a whole 2x2x4 slice. The times are simulated.
32 devices in a mesh: grp: 2 (over y), pipe: 8 (over z, x), head: 2 (over core).
Axes of the slice: x: 2, y: 2, z: 4, core: 2. Of those that a mesh axis runs over, the one named last changes fastest.
Arguments:
- queries: bfloat16 [512, 64, 128], P(('grp', 'pipe'), 'head'), parts along dimension 0, may hold values from -10 to 10
- slice_own_keys: bfloat16 [512, 4, 128], P(('grp', 'pipe'), 'head'), parts along dimension 0, may hold values from -6 to 6
- slice_own_values: bfloat16 [512, 4, 128], P(('grp', 'pipe'), 'head'), parts along dimension 0, may hold values from -6 to 6
- cache_keys: bfloat16 [1664, 4, 128], P(('grp', 'pipe'), 'head'), parts along dimension 0, may hold values from -8 to 8
- context_value_rows: bfloat16 [1664, 4, 128], P(('grp', 'pipe'), 'head'), parts along dimension 0, may hold values from -6 to 6
- prefix_len: int32 [16], P('grp'), parts along dimension 0, may hold values from 1 to 832, as said below
Outputs:
- advanced: bfloat16 [512, 64, 128], P(('grp', 'pipe'), 'head'), parts along dimension 0
There are 2 independent parts, one for each index of `grp`. A program takes and returns all parts, laid end to end along the dimension named above; each array names one. Nothing has to cross between parts.
Inputs may be any that keep to these rules, and one draw needn't show every extreme that they name: prefix_len[p] lies in ((8 - 1 - p) * 104, (8 - p) * 104]; prefix_len[0] is 832 and the last section's is 1.
All inputs are finite; a program needn't handle non-finite values.
Results may differ from a plain program's by a relative error of at most 0.012.
Values may be sent and summed in bfloat16 or wider, within the bound.
A program may use at most 64 MiB of HBM per device.

v0:
```python
import math

import jax
import jax.numpy as jnp
from jax import lax
from jax.sharding import PartitionSpec as P

floor_value = -1e30


def from_behind(value, axis, steps):
    count = lax.axis_size(axis)
    leading, last = (max(0, -steps), min(count, count - steps))
    return lax.ppermute(value, axis, [(source, source + steps) for source in range(leading, last)])


def passed_along(value, axis, steps):
    count = lax.axis_size(axis)
    pairs = [(source, (source + steps) % count) for source in range(count)]
    return lax.ppermute(value, axis, pairs)


def block_scores(grouped, key_block, factor):
    return (
        jnp.einsum("sghd,kgd->gkhs", grouped, key_block, preferred_element_type=jnp.float32)
        * factor
    )


def to_rows(statistic):
    return jnp.transpose(statistic, (2, 0, 1))[..., None]


def absorb(running, scores, value_block, visible):
    weighted, running_max, running_sum = running
    block_max = jnp.max(jnp.where(visible, scores, floor_value), axis=1)
    new_max = jnp.maximum(running_max, block_max)
    weights = jnp.where(visible, jnp.exp(scores - new_max[:, None]), 0.0)
    rescale = jnp.exp(running_max - new_max)
    added = jnp.einsum(
        "gkhs,kgd->sghd",
        weights.astype(jnp.bfloat16),
        value_block,
        preferred_element_type=jnp.float32,
    )
    return (
        weighted * to_rows(rescale) + added,
        new_max,
        running_sum * rescale + jnp.sum(weights, axis=1),
    )


def combine(earlier, later):
    shared_max = jnp.maximum(earlier[1], later[1])
    left_scale = jnp.exp(earlier[1] - shared_max)
    right_scale = jnp.exp(later[1] - shared_max)
    return (
        earlier[0] * to_rows(left_scale) + later[0] * to_rows(right_scale),
        shared_max,
        earlier[2] * left_scale + later[2] * right_scale,
    )


def cache_range(
    running, grouped, whole_keys, whole_values, start_key, stop_key, block_rows, factor
):

    def absorb_block(block_index, carried):
        first_key = block_index * block_rows
        key_block = lax.dynamic_slice_in_dim(whole_keys, first_key, block_rows, 0)
        value_block = lax.dynamic_slice_in_dim(whole_values, first_key, block_rows, 0)
        position = first_key + lax.broadcasted_iota(jnp.int32, (1, block_rows, 1, 1), 1)
        visible = (position >= start_key) & (position < stop_key)
        return absorb(carried, block_scores(grouped, key_block, factor), value_block, visible)

    return lax.fori_loop(
        start_key // block_rows, (stop_key + block_rows - 1) // block_rows, absorb_block, running
    )


def shards(queries, slice_own_keys, slice_own_values, cache_keys, context_value_rows, prefix_len):
    slice_rows, head_count, head_width = queries.shape
    groups = slice_own_keys.shape[1]
    per_group = head_count // groups
    grouped = queries.reshape(slice_rows, groups, per_group, head_width)
    factor = 1.0 / math.sqrt(head_width)
    sections = lax.axis_size("pipe")
    own_index = lax.axis_index("pipe")
    own_prefix = prefix_len[own_index]
    initial = (
        jnp.zeros((slice_rows, groups, per_group, head_width), jnp.float32),
        jnp.full((groups, per_group, slice_rows), floor_value, jnp.float32),
        jnp.zeros((groups, per_group, slice_rows), jnp.float32),
    )
    key_index = lax.broadcasted_iota(jnp.int32, (1, slice_rows, 1, slice_rows), 1)
    row_index = lax.broadcasted_iota(jnp.int32, (1, slice_rows, 1, slice_rows), 3)
    running = absorb(
        initial,
        block_scores(grouped, slice_own_keys, factor),
        slice_own_values,
        key_index <= row_index,
    )
    whole_keys, whole_values = (
        lax.all_gather(cache_keys, "pipe", axis=0, tiled=True),
        lax.all_gather(context_value_rows, "pipe", axis=0, tiled=True),
    )
    context = whole_keys.shape[0]
    block_rows = math.gcd(context, 512)
    half_axis = sections // 2
    lender = own_index < half_axis
    partner_prefix = prefix_len[(own_index + half_axis) % sections]
    source_prefix = prefix_len[(own_index + sections - half_axis) % sections]
    own_cut = (own_prefix + partner_prefix) // 2 // block_rows * block_rows
    lent_cut = (source_prefix + own_prefix) // 2 // block_rows * block_rows
    borrowed = from_behind(grouped, "pipe", half_axis)
    running = cache_range(
        running,
        grouped,
        whole_keys,
        whole_values,
        0,
        jnp.where(lender, own_cut, own_prefix),
        block_rows,
        factor,
    )
    lent_weighted, lent_max, lent_sum = cache_range(
        initial,
        borrowed,
        whole_keys,
        whole_values,
        jnp.where(lender, 0, lent_cut),
        jnp.where(lender, 0, source_prefix),
        block_rows,
        factor,
    )
    returned = (
        from_behind(lent_weighted.astype(jnp.bfloat16), "pipe", -half_axis).astype(
            lent_weighted.dtype
        ),
        from_behind(lent_max.astype(jnp.bfloat16), "pipe", -half_axis).astype(lent_max.dtype),
        from_behind(lent_sum.astype(jnp.bfloat16), "pipe", -half_axis).astype(lent_sum.dtype),
    )
    joined = combine(running, returned)
    running = tuple((jnp.where(lender, merged, kept) for merged, kept in zip(joined, running)))
    weighted, running_max, running_sum = running
    result = (
        (weighted / to_rows(running_sum))
        .astype(jnp.bfloat16)
        .reshape(slice_rows, head_count, head_width)
    )
    return passed_along(result, "pipe", 1)


def solution(mesh):
    in_specs = (
        P(("grp", "pipe"), "head", None),
        P(("grp", "pipe"), "head", None),
        P(("grp", "pipe"), "head", None),
        P(("grp", "pipe"), "head", None),
        P(("grp", "pipe"), "head", None),
        P("grp"),
    )
    out_specs = P(("grp", "pipe"), "head", None)
    return jax.shard_map(shards, mesh=mesh, in_specs=in_specs, out_specs=out_specs, check_vma=False)
```

profile of v0, /device:TPU:0, one launch (start us, length us, event | category | flops | bytes accessed | tf_op | source)
XLA Modules:
  0.0 104.8 jit_solution(3564441653713971423)
XLA Ops:
  0.0 0.0 copy-start
  0.0 1.1 %copy.7 = bf16[32,32,128]{2,0,1:T(8,128)(2,1)S(1)} copy(bf16[32,32,128]{2,1,0:T(8,128)(2,1)} %param.10) | data formatting | bytes 524288 | tf_op args[0]
  1.1 6.0 %collective-permute-start = (bf16[32,2,16,128]{3,0,2,1:T(8,128)(2,1)S(1)}, bf16[32,2,16,128]{3,0,2,1:T(8,128)(2,1)S(1)}, u32[]{:S(2)}, u32[]{:S(2)}) collective-permute-start(bf16[32,2,16,128]{3,0,2,1:T(8,128)(2,1)S(1)} %bitcast.84), channel_id=1, source_target_pairs={{0,8},{2,10},{4,12},{6,14},{1,9},{3,11},{5,13},{7,15},{16,24},{18,... | collective-permute-start | bytes 786440 | tf_op jit(solution)/shard_map/ppermute | solution.py:14
  7.1 0.0 copy-done.1
  7.1 0.0 copy-start.2
  7.1 0.8 copy-done.2
  7.9 0.0 copy-start.3
  7.9 34.2 %all_gather.7 = bf16[832,2,128]{2,0,1:T(8,128)(2,1)S(1)} all-gather(bf16[104,2,128]{2,0,1:T(8,128)(2,1)S(1)} %copy.12), channel_id=1, replica_groups=mesh['grp'=2,'pipe'=8,'head'=2] {'pipe'}, dimensions={0}, use_global_device_ids=true | all-gather | bytes 479232 | tf_op jit(solution)/shard_map/all_gather | solution.py:105
  42.1 0.5 select_reduce_fusion.2
  42.6 0.1 fusion.22
  42.8 31.4 %all_gather.6 = bf16[832,2,128]{2,0,1:T(8,128)(2,1)S(1)} all-gather(bf16[104,2,128]{2,0,1:T(8,128)(2,1)S(1)} %copy.11), channel_id=1, replica_groups=mesh['grp'=2,'pipe'=8,'head'=2] {'pipe'}, dimensions={0}, use_global_device_ids=true | all-gather | bytes 479232 | tf_op jit(solution)/shard_map/all_gather | solution.py:104
  74.2 0.7 copy-done.4
  74.8 0.6 fusion.37
  77.9 0.3 fusion.20
  78.2 0.0 collective-permute-done
  78.2 0.1 broadcast_in_dim.75
  78.3 1.3 %collective-permute-start.1 = (bf16[2,16,32]{2,1,0:T(8,128)(2,1)S(1)}, bf16[2,16,32]{2,1,0:T(8,128)(2,1)S(1)}, u32[]{:S(2)}, u32[]{:S(2)}) collective-permute-start(bf16[2,16,32]{2,1,0:T(8,128)(2,1)S(1)} %convert_element_type.31), channel_id=1, source_target_pairs={{8,0},{10,2},{12,4},{14,6},{9,1},{11,3},{13,5},{15,7},{24,16},{26,... | collective-permute-start | bytes 6152 | tf_op jit(solution)/shard_map/ppermute | solution.py:14
  79.6 1.3 %collective-permute-start.3 = (bf16[2,16,32]{2,1,0:T(8,128)(2,1)S(1)}, bf16[2,16,32]{2,1,0:T(8,128)(2,1)S(1)}, u32[]{:S(2)}, u32[]{:S(2)}) collective-permute-start(bf16[2,16,32]{2,1,0:T(8,128)(2,1)S(1)} %convert_element_type.35), channel_id=1, source_target_pairs={{8,0},{10,2},{12,4},{14,6},{9,1},{11,3},{13,5},{15,7},{24,16},{26,... | collective-permute-start | bytes 6152 | tf_op jit(solution)/shard_map/ppermute | solution.py:14
  81.0 1.3 %collective-permute-start.2 = (bf16[32,2,16,128]{3,0,2,1:T(8,128)(2,1)S(1)}, bf16[32,2,16,128]{3,0,2,1:T(8,128)(2,1)S(1)}, u32[]{:S(2)}, u32[]{:S(2)}) collective-permute-start(bf16[32,2,16,128]{3,0,2,1:T(8,128)(2,1)S(1)} %convert_element_type.33), channel_id=1, source_target_pairs={{8,0},{10,2},{12,4},{14,6},{9,1},{11,3},{13,5},{15,7},{24,16},{26,... | collective-permute-start | bytes 786440 | tf_op jit(solution)/shard_map/ppermute | solution.py:14
  82.3 12.0 %while.28 = (s32[]{:T(128)}, f32[32,2,16,128]{3,0,2,1:T(8,128)S(1)}, f32[2,16,32]{2,1,0:T(8,128)S(1)}, f32[2,16,32]{2,1,0:T(8,128)S(1)}, s32[]{:T(128)}, /*index...) while((s32[]{:T(128)}, ...), condition=%wide.region_5.6_spmd, body=%wide.region_2.5_spmd.sunk | while | flops 34278660 | bytes 3404603 | solution.py:76
  82.3 0.4 select_reduce_fusion.5
  82.7 0.4 fusion.59
  83.1 0.2 fusion.60
  83.3 0.3 multiply_add_fusion.8
  83.6 0.4 select_reduce_fusion.5
  84.0 0.4 fusion.59
  84.5 0.2 fusion.60
  84.7 0.3 multiply_add_fusion.8
  85.0 0.4 select_reduce_fusion.5
  85.4 0.4 fusion.59
  85.8 0.2 fusion.60
  86.0 0.3 multiply_add_fusion.8
  86.3 0.4 select_reduce_fusion.5
  86.7 0.4 fusion.59
  87.1 0.2 fusion.60
  87.3 0.3 multiply_add_fusion.8
  87.7 0.4 select_reduce_fusion.5
  88.0 0.4 fusion.59
  88.5 0.2 fusion.60
  88.7 0.3 multiply_add_fusion.8
  89.0 0.4 select_reduce_fusion.5
  89.4 0.4 fusion.59
  89.8 0.2 fusion.60
  90.0 0.3 multiply_add_fusion.8
  90.3 0.4 select_reduce_fusion.5
  90.7 0.4 fusion.59
  91.1 0.2 fusion.60
  91.3 0.3 multiply_add_fusion.8
  91.7 0.4 select_reduce_fusion.5
  92.0 0.4 fusion.59
  92.5 0.2 fusion.60
  92.7 0.3 multiply_add_fusion.8
  93.0 0.4 select_reduce_fusion.5
  93.4 0.4 fusion.59
  93.8 0.2 fusion.60
  94.0 0.3 multiply_add_fusion.8
  94.3 0.0 collective-permute-done.1
  94.3 0.0 collective-permute-done.3
  94.3 0.0 collective-permute-done.2
  94.4 0.5 divide_convert_fusion
  94.8 0.1 copy.13
  94.9 2.9 %collective-permute-start.4 = (bf16[32,32,128]{2,1,0:T(8,128)(2,1)S(1)}, bf16[32,32,128]{2,1,0:T(8,128)(2,1)S(1)}, u32[]{:S(2)}, u32[]{:S(2)}) collective-permute-start(bf16[32,32,128]{2,1,0:T(8,128)(2,1)S(1)} %bitcast.87), channel_id=1, source_target_pairs={{0,2},{2,4},{4,6},{6,8},{8,10},{10,12},{12,14},{14,0},{1,3},{3,5},... | collective-permute-start | bytes 786440 | tf_op jit(solution)/shard_map/ppermute | solution.py:20
  97.9 6.2 %collective-permute-done.4 = bf16[32,32,128]{2,1,0:T(8,128)(2,1)S(1)} collective-permute-done((bf16[32,32,128]{2,1,0:T(8,128)(2,1)S(1)}, bf16[32,32,128]{2,1,0:T(8,128)(2,1)S(1)}, u32[]{:S(2)}, u32[]{:S(2)}) %collective-permute-start.4) | collective-permute-done | bytes 262176 | tf_op jit(solution)/shard_map/ppermute | solution.py:20
  104.1 0.7 copy.54
  (52 shorter events, 0.4 us)
Async XLA Ops:
  0.0 77.9 %copy-start = (bf16[32,2,128]{2,1,0:T(2,128)(2,1)S(1)}, bf16[32,2,128]{2,1,0:T(2,128)(2,1)}, u32[]{:S(2)}) copy-start(bf16[32,2,128]{2,1,0:T(2,128)(2,1)} %param.12) | copy-start | bytes 49156
  0.0 7.1 %copy-start.1 = (bf16[104,2,128]{2,1,0:T(2,128)(2,1)S(1)}, bf16[104,2,128]{2,1,0:T(2,128)(2,1)}, u32[]{:S(2)}) copy-start(bf16[104,2,128]{2,1,0:T(2,128)(2,1)} %param.13) | copy-start | bytes 159748
  1.1 77.1 %collective-permute-start = (bf16[32,2,16,128]{3,0,2,1:T(8,128)(2,1)S(1)}, bf16[32,2,16,128]{3,0,2,1:T(8,128)(2,1)S(1)}, u32[]{:S(2)}, u32[]{:S(2)}) collective-permute-start(bf16[32,2,16,128]{3,0,2,1:T(8,128)(2,1)S(1)} %bitcast.84), channel_id=1, source_target_pairs={{0,8},{2,10},{4,12},{6,14},{1,9},{3,11},{5,13},{7,15},{16,24},{18,... | collective-permute-start | bytes 786440 | tf_op jit(solution)/shard_map/ppermute | solution.py:14
  7.1 0.8 copy-start.2
  7.9 34.2 %copy-start.3 = (bf16[32,2,128]{2,1,0:T(2,128)(2,1)S(1)}, bf16[32,2,128]{2,1,0:T(2,128)(2,1)}, u32[]{:S(2)}) copy-start(bf16[32,2,128]{2,1,0:T(2,128)(2,1)} %param.11) | copy-start | bytes 49156
  74.2 0.7 copy-start.4
  78.3 16.0 %collective-permute-start.1 = (bf16[2,16,32]{2,1,0:T(8,128)(2,1)S(1)}, bf16[2,16,32]{2,1,0:T(8,128)(2,1)S(1)}, u32[]{:S(2)}, u32[]{:S(2)}) collective-permute-start(bf16[2,16,32]{2,1,0:T(8,128)(2,1)S(1)} %convert_element_type.31), channel_id=1, source_target_pairs={{8,0},{10,2},{12,4},{14,6},{9,1},{11,3},{13,5},{15,7},{24,16},{26,... | collective-permute-start | bytes 6152 | tf_op jit(solution)/shard_map/ppermute | solution.py:14
  79.6 14.7 %collective-permute-start.3 = (bf16[2,16,32]{2,1,0:T(8,128)(2,1)S(1)}, bf16[2,16,32]{2,1,0:T(8,128)(2,1)S(1)}, u32[]{:S(2)}, u32[]{:S(2)}) collective-permute-start(bf16[2,16,32]{2,1,0:T(8,128)(2,1)S(1)} %convert_element_type.35), channel_id=1, source_target_pairs={{8,0},{10,2},{12,4},{14,6},{9,1},{11,3},{13,5},{15,7},{24,16},{26,... | collective-permute-start | bytes 6152 | tf_op jit(solution)/shard_map/ppermute | solution.py:14
  81.0 13.4 %collective-permute-start.2 = (bf16[32,2,16,128]{3,0,2,1:T(8,128)(2,1)S(1)}, bf16[32,2,16,128]{3,0,2,1:T(8,128)(2,1)S(1)}, u32[]{:S(2)}, u32[]{:S(2)}) collective-permute-start(bf16[32,2,16,128]{3,0,2,1:T(8,128)(2,1)S(1)} %convert_element_type.33), channel_id=1, source_target_pairs={{8,0},{10,2},{12,4},{14,6},{9,1},{11,3},{13,5},{15,7},{24,16},{26,... | collective-permute-start | bytes 786440 | tf_op jit(solution)/shard_map/ppermute | solution.py:14
  94.9 9.1 %collective-permute-start.4 = (bf16[32,32,128]{2,1,0:T(8,128)(2,1)S(1)}, bf16[32,32,128]{2,1,0:T(8,128)(2,1)S(1)}, u32[]{:S(2)}, u32[]{:S(2)}) collective-permute-start(bf16[32,32,128]{2,1,0:T(8,128)(2,1)S(1)} %bitcast.87), channel_id=1, source_target_pairs={{0,2},{2,4},{4,6},{6,8},{8,10},{10,12},{12,14},{14,0},{1,3},{3,5},... | collective-permute-start | bytes 786440 | tf_op jit(solution)/shard_map/ppermute | solution.py:20
where the time goes:
time: 105 us
  blocking collectives  65.5 us (62%)
  starting transfers between devices  12.8 us (12%)
  other arithmetic  6.88 us (7%)
  waiting for transfers between devices  6.21 us (6%)
  matrix products  5.96 us (6%)
  local copies, waits for them, and re-layouts  4.04 us (4%)
  between operations  2.71 us (3%)
    all_gather x1, blocking collectives, shards(): lax.all_gather(context_value_rows, 'pipe', axis=0, tiled=True)  34.2 us
    all_gather x1, blocking collectives, shards(): lax.all_gather(cache_keys, 'pipe', axis=0, tiled=True)  31.4 us
    ppermute x4, starting transfers between devices, from_behind(): lax.ppermute(value, axis, [(source, source + steps) for source in range(l...  9.83 us
    ppermute x1, waiting for transfers between devices, passed_along(): return lax.ppermute(value, axis, pairs)  6.2 us
    dot_general x10, matrix products, block_scores(): jnp.einsum('sghd,kgd->gkhs', grouped, key_block, preferred_element_type=j...  3.79 us
    reduce_sum x10, other arithmetic, absorb(): jnp.sum(weights, axis=1)  3.59 us
    unnamed x14, local copies, waits for them, and re-layouts  3.26 us
    ppermute x1, starting transfers between devices, passed_along(): return lax.ppermute(value, axis, pairs)  2.92 us
  transfers between devices with their start and end apart: 5, of which 1 were waited for; matrix products, arithmetic and copies ran while one was open for 12% of the time, Pallas kernels for 0%

commit v1 on v0

v1 whole, which is shorter than its diff:
```python
import functools
import math

import jax
import jax.numpy as jnp
from jax import lax
from jax.experimental import pallas as pl
from jax.experimental.pallas import tpu as pltpu
from jax.sharding import PartitionSpec as P

MESH = pl.DeviceIdType.MESH


def attend_kernel(
    n,
    prefix_ref,
    q_ref,
    own_k_ref,
    own_v_ref,
    key_ref,
    value_ref,
    out_ref,
    kv,
    acc,
    top,
    total,
    stage,
    send_sem,
    recv_sem,
    out_send,
    out_recv,
):
    rows_r = n // 2
    slice_rows, heads, width = q_ref.shape
    groups = kv.shape[1]
    per_group = heads // groups
    columns = slice_rows * per_group
    block = kv.shape[2]
    scale = math.log2(math.e) / math.sqrt(width)
    me = lax.axis_index("pipe")
    z, c = me // 2, me % 2

    barrier = pltpu.get_barrier_semaphore()
    for step in (1, 2, n - 2, n - 1):
        pl.semaphore_signal(
            barrier, inc=1, device_id={"pipe": (me + step) % n}, device_id_type=MESH
        )

    def pick(raw_ref, g):
        count = raw_ref.shape[0] // groups
        row = lax.broadcasted_iota(jnp.int32, (count, count * groups), 0)
        col = lax.broadcasted_iota(jnp.int32, (count, count * groups), 1)
        chosen = jnp.where(col == row * groups + g, 1.0, 0.0).astype(jnp.bfloat16)
        return jnp.dot(chosen, raw_ref[...], preferred_element_type=jnp.float32).astype(
            jnp.bfloat16
        )

    for g in range(groups):
        kv[me, g, :, :width] = pick(key_ref, g)
        kv[me, g, :, width:] = pick(value_ref, g)
    pl.semaphore_wait(barrier, 4)

    def copy(direction, b, g, target):
        return pltpu.make_async_remote_copy(
            src_ref=kv.at[b, g],
            dst_ref=kv.at[b, g],
            send_sem=send_sem.at[direction, b, g],
            recv_sem=recv_sem.at[b, g],
            device_id={"pipe": target},
            device_id_type=MESH,
        )

    def down_if(zb):
        return (zb >= z) & (zb < rows_r) & (z > 0)

    def up_if(zb):
        return (zb >= 0) & (zb <= z) & (z + 1 <= rows_r - 1 - zb)

    def across_if(zb):
        return (zb >= 0) & (zb < rows_r) & (z <= rows_r - 1 - zb)

    def sends(zb, act, downward, upward):
        b = zb * 2 + c
        for g in range(groups):
            if downward:

                @pl.when(down_if(zb))
                def _():
                    act(copy(0, b, g, me - 2))

            if upward:

                @pl.when(up_if(zb))
                def _():
                    act(copy(1, b, g, me + 2))

            @pl.when(across_if(zb))
            def _():
                act(copy(2, b, g, z * 2 + 1 - c))

    sends(z, lambda dma: dma.start(), True, True)

    def query(g):
        return q_ref[:, g * per_group : (g + 1) * per_group, :].reshape(columns, width)

    def scores(keys, g):
        return lax.dot_general(
            keys, query(g), (((1,), (1,)), ((), ())), preferred_element_type=jnp.float32
        )

    def gather(values, weights):
        return lax.dot_general(
            values,
            weights.astype(jnp.bfloat16),
            (((0,), (0,)), ((), ())),
            preferred_element_type=jnp.float32,
        )

    for g in range(groups):
        s = scores(pick(own_k_ref, g), g)
        key_index = lax.broadcasted_iota(jnp.int32, s.shape, 0)
        row_index = lax.broadcasted_iota(jnp.int32, s.shape, 1) // per_group
        s = jnp.where(key_index <= row_index, s, -1e30)
        m = jnp.max(s, axis=0, keepdims=True)
        w = jnp.exp2((s - m) * scale)
        top[g] = m
        total[g] = jnp.sum(w, axis=0, keepdims=True)
        acc[g] = gather(pick(own_v_ref, g), w)

    prefix = prefix_ref[me]

    def absorb(b, g):
        s = scores(kv[b, g, :, :width], g)
        key_index = lax.broadcasted_iota(jnp.int32, s.shape, 0)
        s = jnp.where(key_index < prefix - b * block, s, -1e30)
        old = top[g]
        m = jnp.maximum(old, jnp.max(s, axis=0, keepdims=True))
        w = jnp.exp2((s - m) * scale)
        fade = jnp.exp2((old - m) * scale)
        top[g] = m
        total[g] = total[g] * fade + jnp.sum(w, axis=0, keepdims=True)
        acc[g] = acc[g] * fade + gather(kv[b, g, :, width:], w)

    def wait_recv(b, g):
        copy(0, b, g, me).wait_recv()

    def from_above(d):
        return (d > 0) & (z + d < rows_r)

    def from_below(d):
        return (d > 0) & (z - d >= 0) & (z <= rows_r - 1 - (z - d))

    def step(d, carry):
        @pl.when(from_above(d))
        def _():
            for g in range(groups):
                wait_recv((z + d) * 2 + c, g)
            sends(z + d, lambda dma: dma.start(), True, False)

        @pl.when(from_below(d))
        def _():
            for g in range(groups):
                wait_recv((z - d) * 2 + c, g)
            sends(z - d, lambda dma: dma.start(), False, True)

        def use(j, inner):
            crossing = j // 2
            sign = 1 - 2 * (j % 2)
            reach = d - crossing
            zb = z + sign * reach
            b = zb * 2 + jnp.where(crossing == 1, 1 - c, c)
            there = (reach >= 0) & (zb >= 0) & (zb < rows_r) & ((reach > 0) | (sign > 0))
            needed = there & (b <= n - 1 - me)

            @pl.when(needed)
            def _():
                @pl.when(crossing == 1)
                def _():
                    for g in range(groups):
                        wait_recv(b, g)

                for g in range(groups):
                    absorb(b, g)

            return inner

        lax.fori_loop(0, 4, use, 0)
        return carry

    lax.fori_loop(0, rows_r + 1, step, 0)

    outs = []
    for g in range(groups):
        done = jnp.transpose(acc[g] / total[g])
        part = pl.ds(g * per_group, per_group)
        stage[:, part, :] = done.astype(jnp.bfloat16).reshape(slice_rows, per_group, width)
        dma = pltpu.make_async_remote_copy(
            src_ref=stage.at[:, part, :],
            dst_ref=out_ref.at[:, part, :],
            send_sem=out_send.at[g],
            recv_sem=out_recv.at[g],
            device_id={"pipe": (me + 1) % n},
            device_id_type=MESH,
        )
        dma.start()
        outs.append(dma)

    def drain(d, carry):
        @pl.when(from_above(d))
        def _():
            sends(z + d, lambda dma: dma.wait_send(), True, False)

        @pl.when(from_below(d))
        def _():
            sends(z - d, lambda dma: dma.wait_send(), False, True)

        return carry

    sends(z, lambda dma: dma.wait_send(), True, True)
    lax.fori_loop(1, rows_r, drain, 0)
    for dma in outs:
        dma.wait()


def fused(queries, slice_own_keys, slice_own_values, cache_keys, context_value_rows, prefix_len):
    n = lax.axis_size("pipe")
    slice_rows, heads, width = queries.shape
    block, groups, _ = cache_keys.shape
    columns = slice_rows * heads // groups
    vmem = pl.BlockSpec(memory_space=pltpu.VMEM)
    return pl.pallas_call(
        functools.partial(attend_kernel, n),
        out_shape=jax.ShapeDtypeStruct(queries.shape, jnp.bfloat16),
        in_specs=[pl.BlockSpec(memory_space=pltpu.SMEM)] + [vmem] * 5,
        out_specs=vmem,
        scratch_shapes=[
            pltpu.VMEM((n, groups, block, 2 * width), jnp.bfloat16),
            pltpu.VMEM((groups, width, columns), jnp.float32),
            pltpu.VMEM((groups, 1, columns), jnp.float32),
            pltpu.VMEM((groups, 1, columns), jnp.float32),
            pltpu.VMEM(queries.shape, jnp.bfloat16),
            pltpu.SemaphoreType.DMA((3, n, groups)),
            pltpu.SemaphoreType.DMA((n, groups)),
            pltpu.SemaphoreType.DMA((groups,)),
            pltpu.SemaphoreType.DMA((groups,)),
        ],
        compiler_params=pltpu.CompilerParams(
            collective_id=0, has_side_effects=True, vmem_limit_bytes=40 * 1024 * 1024
        ),
        name="relay_attention",
    )(
        prefix_len,
        queries,
        slice_own_keys.reshape(-1, width),
        slice_own_values.reshape(-1, width),
        cache_keys.reshape(-1, width),
        context_value_rows.reshape(-1, width),
    )


def solution(mesh):
    in_specs = (
        P(("grp", "pipe"), "head", None),
        P(("grp", "pipe"), "head", None),
        P(("grp", "pipe"), "head", None),
        P(("grp", "pipe"), "head", None),
        P(("grp", "pipe"), "head", None),
        P("grp"),
    )
    out_specs = P(("grp", "pipe"), "head", None)
    return jax.shard_map(fused, mesh=mesh, in_specs=in_specs, out_specs=out_specs, check_vma=False)
```

time: 105 us -> 36.1 us (0.34)
  blocking collectives: 65.5 us -> 0 us
  Pallas kernels: 0 us -> 30.3 us
  starting transfers between devices: 12.8 us -> 0 us
  other arithmetic: 6.88 us -> 0 us
  waiting for transfers between devices: 6.21 us -> 0 us
  matrix products: 5.96 us -> 0 us
  between operations: 2.71 us -> 0.02 us
  local copies, waits for them, and re-layouts: 4.04 us -> 5.36 us
    all_gather x2 -> x0, blocking collectives: 65.5 us -> none  [the longest x1 34.2 us: shards(): lax.all_gather(context_value_rows, 'pipe', axis=0, tiled=True)]
    pallas_call x0 -> x1, Pallas kernels: none -> 30.3 us  [fused(): pl.pallas_call(functools.partial(attend_kernel, n), out_shape=jax.ShapeDt...]
    ppermute x5 -> x0, starting transfers between devices: 12.8 us -> none  [the longest x4 9.83 us: from_behind(): lax.ppermute(value, axis, [(source, source + steps) for source in range(l...]
    ppermute x5 -> x0, waiting for transfers between devices: 6.21 us -> none  [the longest x1 6.2 us: passed_along(): return lax.ppermute(value, axis, pairs)]
    dot_general x11 -> x0, matrix products: 4.1 us -> none  [the longest x10 3.79 us: block_scores(): jnp.einsum('sghd,kgd->gkhs', grouped, key_block, preferred_element_type=j...]
    reduce_sum x10 -> x0, other arithmetic: 3.59 us -> none  [absorb(): jnp.sum(weights, axis=1)]
    add x19 -> x0, other arithmetic: 2.56 us -> none  [the longest x9 2.43 us: absorb(): weighted * to_rows(rescale) + added]
    unnamed x14 -> x13, local copies, waits for them, and re-layouts: 3.26 us -> 5.36 us
  transfers between devices with their start and end apart: 5 -> 0, of which waited for: 1 -> 0; matrix products, arithmetic and copies ran while one was open for 12% -> 0% of each run, Pallas kernels for 0% -> 0%
where the time goes in v1:
time: 36.1 us; the launch traced here: 35.7 us
  Pallas kernels  30.3 us (84%)
  local copies, waits for them, and re-layouts  5.36 us (15%)
    pallas_call x1, Pallas kernels, fused(): pl.pallas_call(functools.partial(attend_kernel, n), out_shape=jax.ShapeDt...  30.3 us
    unnamed x13, local copies, waits for them, and re-layouts  5.36 us

profile of v1, /device:TPU:0, one launch (start us, length us, event | category | flops | bytes accessed | tf_op | source)
XLA Modules:
  0.0 35.7 jit_solution(2688767527253236394)
XLA Ops:
  0.0 0.0 copy-start.5
  0.0 0.7 %copy-done.5 = s32[8]{0:T(128)S(1)} copy-done((s32[8]{0:T(128)S(1)}, s32[8]{0:T(128)}, u32[]{:S(2)}) %copy-start.5) | copy-done | bytes 56
  0.7 0.0 copy-start
  0.7 0.9 %copy-done = bf16[32,32,128]{2,1,0:T(8,128)(2,1)S(1)} copy-done((bf16[32,32,128]{2,1,0:T(8,128)(2,1)S(1)}, bf16[32,32,128]{2,1,0:T(8,128)(2,1)}, u32[]{:S(2)}) %copy-start) | copy-done | bytes 262168
  1.6 0.0 copy-start.1
  1.6 0.8 %copy-done.1 = bf16[104,2,128]{2,1,0:T(2,128)(2,1)S(1)} copy-done((bf16[104,2,128]{2,1,0:T(2,128)(2,1)S(1)}, bf16[104,2,128]{2,1,0:T(2,128)(2,1)}, u32[]{:S(2)}) %copy-start.1) | copy-done | bytes 53272
  2.4 0.0 copy-start.2
  2.4 0.8 %copy-done.2 = bf16[104,2,128]{2,1,0:T(2,128)(2,1)S(1)} copy-done((bf16[104,2,128]{2,1,0:T(2,128)(2,1)S(1)}, bf16[104,2,128]{2,1,0:T(2,128)(2,1)}, u32[]{:S(2)}) %copy-start.2) | copy-done | bytes 53272
  3.2 0.0 copy-start.3
  3.2 0.7 %copy-done.3 = bf16[32,2,128]{2,1,0:T(2,128)(2,1)S(1)} copy-done((bf16[32,2,128]{2,1,0:T(2,128)(2,1)S(1)}, bf16[32,2,128]{2,1,0:T(2,128)(2,1)}, u32[]{:S(2)}) %copy-start.3) | copy-done | bytes 16408
  3.9 0.0 copy-start.4
  3.9 0.7 %copy-done.4 = bf16[32,2,128]{2,1,0:T(2,128)(2,1)S(1)} copy-done((bf16[32,2,128]{2,1,0:T(2,128)(2,1)S(1)}, bf16[32,2,128]{2,1,0:T(2,128)(2,1)}, u32[]{:S(2)}) %copy-start.4) | copy-done | bytes 16408
  4.7 30.3 %relay_attention.1 = bf16[32,32,128]{2,1,0:T(8,128)(2,1)S(1)} custom-call(s32[8]{0:T(128)S(1)} %copy-done.5, bf16[32,32,128]{2,1,0:T(8,128)(2,1)S(1)} %copy-done, bf16[64,128]{1,0:T(8,128)(2,1)S(1)} %bitcast.6, bf16[64,128]{1,0:T(8,128)(2,1)S(1)} %bitcast.7, bf16[208,128]{1,0:T(8,128)(2,1)S(1)} %bitcast.4, bf16[208,128]{1,0:T(8,128)(2,1)S(1)} %bitcast.5), custom_call_target="tpu_custom_call" | custom-call | tf_op jit(solution)/shard_map/relay_attention/pallas_call | solution.py:231
  35.0 0.7 %copy.8 = bf16[32,32,128]{2,1,0:T(8,128)(2,1)} copy(bf16[32,32,128]{2,1,0:T(8,128)(2,1)S(1)} %relay_attention.1) | data formatting | bytes 524288
Async XLA Ops:
  0.0 0.7 %copy-start.5 = (s32[8]{0:T(128)S(1)}, s32[8]{0:T(128)}, u32[]{:S(2)}) copy-start(s32[8]{0:T(128)} %prefix_ref.1) | copy-start | bytes 100
  0.7 0.9 %copy-start = (bf16[32,32,128]{2,1,0:T(8,128)(2,1)S(1)}, bf16[32,32,128]{2,1,0:T(8,128)(2,1)}, u32[]{:S(2)}) copy-start(bf16[32,32,128]{2,1,0:T(8,128)(2,1)} %q_ref.1) | copy-start | bytes 786436
  1.6 0.8 %copy-start.1 = (bf16[104,2,128]{2,1,0:T(2,128)(2,1)S(1)}, bf16[104,2,128]{2,1,0:T(2,128)(2,1)}, u32[]{:S(2)}) copy-start(bf16[104,2,128]{2,1,0:T(2,128)(2,1)} %param.9) | copy-start | bytes 159748
  2.4 0.8 %copy-start.2 = (bf16[104,2,128]{2,1,0:T(2,128)(2,1)S(1)}, bf16[104,2,128]{2,1,0:T(2,128)(2,1)}, u32[]{:S(2)}) copy-start(bf16[104,2,128]{2,1,0:T(2,128)(2,1)} %param.10) | copy-start | bytes 159748
  3.2 0.7 %copy-start.3 = (bf16[32,2,128]{2,1,0:T(2,128)(2,1)S(1)}, bf16[32,2,128]{2,1,0:T(2,128)(2,1)}, u32[]{:S(2)}) copy-start(bf16[32,2,128]{2,1,0:T(2,128)(2,1)} %param.7) | copy-start | bytes 49156
  3.9 0.7 %copy-start.4 = (bf16[32,2,128]{2,1,0:T(2,128)(2,1)S(1)}, bf16[32,2,128]{2,1,0:T(2,128)(2,1)}, u32[]{:S(2)}) copy-start(bf16[32,2,128]{2,1,0:T(2,128)(2,1)} %param.8) | copy-start | bytes 49156

commit v2 on v1

--- a/solution.py
+++ b/solution.py
@@ -13,14 +13,22 @@
 
 def attend_kernel(
     n,
+    prefix_hbm,
+    q_hbm,
+    own_k_hbm,
+    own_v_hbm,
+    key_hbm,
+    value_hbm,
+    out_ref,
     prefix_ref,
     q_ref,
     own_k_ref,
     own_v_ref,
     key_ref,
     value_ref,
-    out_ref,
+    load_sem,
     kv,
+    turned,
     acc,
     top,
     total,
@@ -40,6 +48,21 @@
     me = lax.axis_index("pipe")
     z, c = me // 2, me % 2
 
+    loads = [
+        pltpu.make_async_copy(source, target, load_sem.at[i])
+        for i, (source, target) in enumerate(
+            (
+                (key_hbm, key_ref),
+                (value_hbm, value_ref),
+                (own_k_hbm, own_k_ref),
+                (own_v_hbm, own_v_ref),
+                (q_hbm, q_ref),
+                (prefix_hbm, prefix_ref),
+            )
+        )
+    ]
+    for load in loads:
+        load.start()
     barrier = pltpu.get_barrier_semaphore()
     for step in (1, 2, n - 2, n - 1):
         pl.semaphore_signal(
@@ -55,6 +78,8 @@
             jnp.bfloat16
         )
 
+    loads[0].wait()
+    loads[1].wait()
     for g in range(groups):
         kv[me, g, :, :width] = pick(key_ref, g)
         kv[me, g, :, width:] = pick(value_ref, g)
@@ -79,34 +104,38 @@
     def across_if(zb):
         return (zb >= 0) & (zb < rows_r) & (z <= rows_r - 1 - zb)
 
-    def sends(zb, act, downward, upward):
+    def sends(zb, g, act, downward, upward):
         b = zb * 2 + c
-        for g in range(groups):
-            if downward:
-
-                @pl.when(down_if(zb))
-                def _():
-                    act(copy(0, b, g, me - 2))
-
-            if upward:
-
-                @pl.when(up_if(zb))
-                def _():
-                    act(copy(1, b, g, me + 2))
-
-            @pl.when(across_if(zb))
-            def _():
-                act(copy(2, b, g, z * 2 + 1 - c))
-
-    sends(z, lambda dma: dma.start(), True, True)
+        if downward:
+
+            @pl.when(down_if(zb))
+            def _():
+                act(copy(0, b, g, me - 2))
+
+        if upward:
+
+            @pl.when(up_if(zb))
+            def _():
+                act(copy(1, b, g, me + 2))
+
+        @pl.when(across_if(zb))
+        def _():
+            act(copy(2, b, g, z * 2 + 1 - c))
+
+    for g in range(groups):
+        sends(z, g, lambda dma: dma.start(), True, True)
+
+    for load in loads[2:]:
+        load.wait()
 
     def query(g):
         return q_ref[:, g * per_group : (g + 1) * per_group, :].reshape(columns, width)
 
+    for g in range(groups):
+        turned[g] = jnp.transpose(query(g))
+
     def scores(keys, g):
-        return lax.dot_general(
-            keys, query(g), (((1,), (1,)), ((), ())), preferred_element_type=jnp.float32
-        )
+        return jnp.dot(keys, turned[g], preferred_element_type=jnp.float32)
 
     def gather(values, weights):
         return lax.dot_general(
@@ -151,17 +180,17 @@
         return (d > 0) & (z - d >= 0) & (z <= rows_r - 1 - (z - d))
 
     def step(d, carry):
-        @pl.when(from_above(d))
-        def _():
-            for g in range(groups):
+        for g in range(groups):
+
+            @pl.when(from_above(d))
+            def _():
                 wait_recv((z + d) * 2 + c, g)
-            sends(z + d, lambda dma: dma.start(), True, False)
-
-        @pl.when(from_below(d))
-        def _():
-            for g in range(groups):
+                sends(z + d, g, lambda dma: dma.start(), True, False)
+
+            @pl.when(from_below(d))
+            def _():
                 wait_recv((z - d) * 2 + c, g)
-            sends(z - d, lambda dma: dma.start(), False, True)
+                sends(z - d, g, lambda dma: dma.start(), False, True)
 
         def use(j, inner):
             crossing = j // 2
@@ -206,17 +235,20 @@
         outs.append(dma)
 
     def drain(d, carry):
-        @pl.when(from_above(d))
-        def _():
-            sends(z + d, lambda dma: dma.wait_send(), True, False)
-
-        @pl.when(from_below(d))
-        def _():
-            sends(z - d, lambda dma: dma.wait_send(), False, True)
+        for g in range(groups):
+
+            @pl.when(from_above(d))
+            def _():
+                sends(z + d, g, lambda dma: dma.wait_send(), True, False)
+
+            @pl.when(from_below(d))
+            def _():
+                sends(z - d, g, lambda dma: dma.wait_send(), False, True)
 
         return carry
 
-    sends(z, lambda dma: dma.wait_send(), True, True)
+    for g in range(groups):
+        sends(z, g, lambda dma: dma.wait_send(), True, True)
     lax.fori_loop(1, rows_r, drain, 0)
     for dma in outs:
         dma.wait()
@@ -227,14 +259,21 @@
     slice_rows, heads, width = queries.shape
     block, groups, _ = cache_keys.shape
     columns = slice_rows * heads // groups
-    vmem = pl.BlockSpec(memory_space=pltpu.VMEM)
     return pl.pallas_call(
         functools.partial(attend_kernel, n),
         out_shape=jax.ShapeDtypeStruct(queries.shape, jnp.bfloat16),
-        in_specs=[pl.BlockSpec(memory_space=pltpu.SMEM)] + [vmem] * 5,
-        out_specs=vmem,
+        in_specs=[pl.BlockSpec(memory_space=pltpu.HBM)] * 6,
+        out_specs=pl.BlockSpec(memory_space=pltpu.VMEM),
         scratch_shapes=[
+            pltpu.SMEM(prefix_len.shape, jnp.int32),
+            pltpu.VMEM(queries.shape, jnp.bfloat16),
+            pltpu.VMEM((slice_rows * groups, width), jnp.bfloat16),
+            pltpu.VMEM((slice_rows * groups, width), jnp.bfloat16),
+            pltpu.VMEM((block * groups, width), jnp.bfloat16),
+            pltpu.VMEM((block * groups, width), jnp.bfloat16),
+            pltpu.SemaphoreType.DMA((6,)),
             pltpu.VMEM((n, groups, block, 2 * width), jnp.bfloat16),
+            pltpu.VMEM((groups, width, columns), jnp.bfloat16),
             pltpu.VMEM((groups, width, columns), jnp.float32),
             pltpu.VMEM((groups, 1, columns), jnp.float32),
             pltpu.VMEM((groups, 1, columns), jnp.float32),
@@ -245,7 +284,7 @@
             pltpu.SemaphoreType.DMA((groups,)),
         ],
         compiler_params=pltpu.CompilerParams(
-            collective_id=0, has_side_effects=True, vmem_limit_bytes=40 * 1024 * 1024
+            collective_id=0, has_side_effects=True, vmem_limit_bytes=63 * 1024 * 1024
         ),
         name="relay_attention",
     )(

time: 36.1 us -> 30.6 us (0.85)
  local copies, waits for them, and re-layouts: 5.36 us -> 1.67 us
  Pallas kernels: 30.3 us -> 28.7 us
    unnamed x13 -> x1, local copies, waits for them, and re-layouts: 5.36 us -> 1.67 us
    pallas_call x1, Pallas kernels: 30.3 us -> 28.7 us  [fused(): pl.pallas_call(functools.partial(attend_kernel, n), out_shape=jax.ShapeDt...]
where the time goes in v2:
time: 30.6 us; the launch traced here: 30.4 us
  Pallas kernels  28.7 us (94%)
  local copies, waits for them, and re-layouts  1.67 us (5%)
    pallas_call x1, Pallas kernels, fused(): pl.pallas_call(functools.partial(attend_kernel, n), out_shape=jax.ShapeDt...  28.7 us
    unnamed x1, local copies, waits for them, and re-layouts  1.67 us

profile of v2, /device:TPU:0, one launch (start us, length us, event | category | flops | bytes accessed | tf_op | source)
XLA Modules:
  0.0 30.4 jit_solution(14173693940803420108)
XLA Ops:
  0.0 28.7 %relay_attention.1 = bf16[32,32,128]{2,1,0:T(8,128)(2,1)} custom-call(s32[8]{0:T(128)} %prefix_hbm.1, bf16[32,32,128]{2,1,0:T(8,128)(2,1)} %q_hbm.1, bf16[64,128]{1,0:T(8,128)(2,1)} %bitcast.6, bf16[64,128]{1,0:T(8,128)(2,1)} %bitcast.7, bf16[208,128]{1,0:T(8,128)(2,1)} %bitcast.4, bf16[208,128]{1,0:T(8,128)(2,1)} %bitcast.5), custom_call_target="tpu_custom_call" | custom-call | tf_op jit(solution)/shard_map/relay_attention/pallas_call | solution.py:262
  28.7 1.7 %copy.8 = bf16[32,32,128]{2,1,0:T(8,128)(2,1)} copy(bf16[32,32,128]{2,1,0:T(8,128)(2,1)} %relay_attention.1) | data formatting | bytes 524288

commit v3 on v2

--- a/solution.py
+++ b/solution.py
@@ -216,23 +216,36 @@
         lax.fori_loop(0, 4, use, 0)
         return carry
 
-    lax.fori_loop(0, rows_r + 1, step, 0)
-
-    outs = []
-    for g in range(groups):
+    lax.fori_loop(0, rows_r, step, 0)
+
+    def leave(g, source, target, sems, target_ref):
+        part = pl.ds(g * per_group, per_group)
+        return pltpu.make_async_remote_copy(
+            src_ref=source.at[:, part, :],
+            dst_ref=target_ref.at[:, part, :],
+            send_sem=sems[0].at[g],
+            recv_sem=sems[1].at[g],
+            device_id={"pipe": target},
+            device_id_type=MESH,
+        )
+
+    def direct(g):
+        return leave(g, stage, (me + 1) % n, (out_send, out_recv), out_ref)
+
+    far = rows_r - 1 - z
+    far_block = far * 2 + 1 - c
+    for g in range(groups):
+
+        @pl.when((z == 0) | (z == rows_r - 1))
+        def _():
+            wait_recv(far_block, g)
+            absorb(far_block, g)
+
         done = jnp.transpose(acc[g] / total[g])
         part = pl.ds(g * per_group, per_group)
         stage[:, part, :] = done.astype(jnp.bfloat16).reshape(slice_rows, per_group, width)
-        dma = pltpu.make_async_remote_copy(
-            src_ref=stage.at[:, part, :],
-            dst_ref=out_ref.at[:, part, :],
-            send_sem=out_send.at[g],
-            recv_sem=out_recv.at[g],
-            device_id={"pipe": (me + 1) % n},
-            device_id_type=MESH,
-        )
-        dma.start()
-        outs.append(dma)
+
+        direct(g).start()
 
     def drain(d, carry):
         for g in range(groups):
@@ -250,8 +263,8 @@
     for g in range(groups):
         sends(z, g, lambda dma: dma.wait_send(), True, True)
     lax.fori_loop(1, rows_r, drain, 0)
-    for dma in outs:
-        dma.wait()
+    for g in range(groups):
+        direct(g).wait()
 
 
 def fused(queries, slice_own_keys, slice_own_values, cache_keys, context_value_rows, prefix_len):

time: 30.6 us -> 29.4 us (0.961)
  Pallas kernels: 28.7 us -> 27.6 us
    pallas_call x1, Pallas kernels: 28.7 us -> 27.6 us  [fused(): pl.pallas_call(functools.partial(attend_kernel, n), out_shape=jax.ShapeDt...]
where the time goes in v3:
time: 29.4 us; the launch traced here: 29.3 us
  Pallas kernels  27.6 us (94%)
  local copies, waits for them, and re-layouts  1.67 us (6%)
    pallas_call x1, Pallas kernels, fused(): pl.pallas_call(functools.partial(attend_kernel, n), out_shape=jax.ShapeDt...  27.6 us
    unnamed x1, local copies, waits for them, and re-layouts  1.67 us

profile of v3, /device:TPU:0, one launch (start us, length us, event | category | flops | bytes accessed | tf_op | source)
XLA Modules:
  0.0 29.3 jit_solution(10509284623033759778)
XLA Ops:
  0.0 27.6 %relay_attention.1 = bf16[32,32,128]{2,1,0:T(8,128)(2,1)} custom-call(s32[8]{0:T(128)} %prefix_hbm.1, bf16[32,32,128]{2,1,0:T(8,128)(2,1)} %q_hbm.1, bf16[64,128]{1,0:T(8,128)(2,1)} %bitcast.6, bf16[64,128]{1,0:T(8,128)(2,1)} %bitcast.7, bf16[208,128]{1,0:T(8,128)(2,1)} %bitcast.4, bf16[208,128]{1,0:T(8,128)(2,1)} %bitcast.5), custom_call_target="tpu_custom_call" | custom-call | tf_op jit(solution)/shard_map/relay_attention/pallas_call | solution.py:275
  27.6 1.7 %copy.8 = bf16[32,32,128]{2,1,0:T(8,128)(2,1)} copy(bf16[32,32,128]{2,1,0:T(8,128)(2,1)} %relay_attention.1) | data formatting | bytes 524288
